TPU v7x, 256 devices: a whole 4x4x8 slice. The times are simulated.
256 devices in a mesh: freq: 16 (over x, y_lo, core), rcv: 16 (over z, y_hi).
Axes of the slice: x: 4, y: 4 (y_hi: 2, y_lo: 2; y = y_hi * 2 + y_lo), z: 8, core: 2. Of those that a mesh axis runs over, the one named last changes fastest.
Arguments:
- reflection: bfloat16 [2, 32, 4096, 4096], P(None, 'freq', 'rcv'), may hold values from -1 to 1, as said below
- focus_plus: bfloat16 [2, 32, 128, 4096], P(None, 'freq', None, 'rcv'), may hold values from -6 to 6
- focus_direct: bfloat16 [2, 32, 128, 4096], P(None, 'freq', None, 'rcv'), may hold values from -6 to 6
- arrival: int32 [128, 4096], P(None, 'rcv'), may hold values from 2 to 31
Outputs:
- focus_minus: bfloat16 [2, 32, 128, 4096], P(None, 'freq', None, 'rcv')
- focus_next: bfloat16 [2, 32, 128, 4096], P(None, 'freq', None, 'rcv')
Inputs may be any that keep to these rules, and one draw needn't show every extreme that they name: reflection is reciprocal: reflection[c, k, r, s] equals reflection[c, k, s, r] for all components, frequencies and positions.
All inputs are finite; a program needn't handle non-finite values.
Results may differ from a plain program's by a relative error of at most 0.0056.
Values may be sent and summed in bfloat16 or wider, within the bound.
A program may use at most 64 MiB of HBM per device.

v0:
```python
import jax
import jax.numpy as jnp
from jax import lax
from jax.sharding import PartitionSpec as P

highest = lax.Precision.HIGHEST


def tables(freq_count, time_count):
    frequency = jnp.arange(freq_count, dtype=jnp.int32)
    sample = jnp.arange(time_count, dtype=jnp.int32)
    phase = sample[:, None] * frequency[None, :] % time_count
    angle = phase.astype(jnp.float32) * (2.0 * jnp.pi / time_count)
    return (jnp.cos(angle), jnp.sin(angle))


def windowed(spectrum, arrival):
    freq_count = spectrum.shape[1]
    time_count = 2 * freq_count
    cosine_table, sine_table = tables(freq_count, time_count)
    real_part = spectrum[0].astype(jnp.float32).reshape(freq_count, -1)
    imag_part = spectrum[1].astype(jnp.float32).reshape(freq_count, -1)
    traces = (
        jnp.dot(cosine_table, real_part, precision=highest)
        - jnp.dot(sine_table, imag_part, precision=highest)
    ) / freq_count
    traces = traces.reshape((time_count,) + spectrum.shape[2:])
    sample = jnp.arange(time_count, dtype=jnp.int32)[:, None, None]
    inside = (sample < arrival[None]) | (sample > time_count - arrival[None])
    masked = jnp.where(inside, traces, jnp.float32(0.0)).reshape(time_count, -1)
    back_real = jnp.dot(cosine_table.T, masked, precision=highest)
    back_imag = -jnp.dot(sine_table.T, masked, precision=highest)
    return jnp.stack([back_real, back_imag]).reshape(spectrum.shape).astype(jnp.bfloat16)


def product(left, right, pattern):
    return jnp.einsum(pattern, left, right, preferred_element_type=jnp.float32)


def time_window(spectrum, arrival):
    shuffled = lax.all_to_all(spectrum, "freq", split_axis=2, concat_axis=1, tiled=True)
    focal_block = shuffled.shape[2]
    offset = lax.axis_index("freq") * focal_block
    local_arrival = lax.dynamic_slice_in_dim(arrival, offset, focal_block, 0)
    return lax.all_to_all(
        windowed(shuffled, local_arrival), "freq", split_axis=1, concat_axis=2, tiled=True
    )


def local(reflection, focus_plus, focus_direct, arrival):
    refl_real = reflection[0]
    refl_imag = reflection[1]
    segment = lax.all_gather(focus_plus, "rcv", axis=3, tiled=True)
    part_real = refl_real
    part_imag = refl_imag
    pattern = "fps,frs->fpr"
    real_total = product(segment[0], part_real, pattern) - product(segment[1], part_imag, pattern)
    imag_total = product(segment[1], part_real, pattern) + product(segment[0], part_imag, pattern)
    upgoing = jnp.stack([real_total, imag_total]).astype(jnp.bfloat16)
    focus_minus = time_window(upgoing, arrival)
    part_real = refl_real
    part_imag = refl_imag
    pattern = "fpr,frs->sfp"
    real_term = product(focus_minus[0], part_real, pattern) + product(
        focus_minus[1], part_imag, pattern
    )
    imag_term = product(focus_minus[1], part_real, pattern) - product(
        focus_minus[0], part_imag, pattern
    )
    summed = lax.psum_scatter(
        jnp.stack([real_term, imag_term], axis=1), "rcv", scatter_dimension=0, tiled=True
    )
    downgoing = jnp.transpose(summed, (1, 2, 3, 0)).astype(jnp.bfloat16)
    correction = time_window(downgoing, arrival)
    focus_next = (focus_direct.astype(jnp.float32) + correction.astype(jnp.float32)).astype(
        jnp.bfloat16
    )
    return (focus_minus, focus_next)


def solution(mesh):
    return jax.shard_map(
        local,
        mesh=mesh,
        in_specs=(
            P(None, "freq", "rcv", None),
            P(None, "freq", None, "rcv"),
            P(None, "freq", None, "rcv"),
            P(None, "rcv"),
        ),
        out_specs=(P(None, "freq", None, "rcv"), P(None, "freq", None, "rcv")),
        check_vma=False,
    )
```

profile of v0, /device:TPU:1, one launch (start us, length us, event | category | flops | bytes accessed | tf_op | source)
XLA Modules:
  0.0 423.8 jit_solution(15329244207024518242)
XLA Ops:
  7.2 0.7 all-gather.2.cloned.1.call-update
  7.9 108.3 %all-gather.2.cloned.1.call-done = bf16[2,2,128,4096]{3,2,1,0:T(8,128)(2,1)} async-done(((bf16[2,2,128,256]{3,2,1,0:T(8,128)(2,1)}), bf16[2,2,128,4096]{3,2,1,0:T(8,128)(2,1)}) %all-gather.2.cloned.1.call-update) | async-done | bytes 4194320 | tf_op jit(solution)/shard_map/all_gather | solution.py:53
  116.2 4.5 %fusion.4 = f32[2,128,256]{2,1,0:T(8,128)S(1)} fusion(bf16[2,2,256,4096]{3,2,1,0:T(8,128)(2,1)} %param.4, bf16[2,2,128,4096]{3,2,1,0:T(8,128)(2,1)} %all-gather.2.cloned.1.call-done), kind=kOutput, calls=%fused_computation.7 | convolution fusion | flops 536870912 | bytes 6553600 | tf_op jit(solution)/shard_map/fps,frs->fpr/dot_general | solution.py:37
  120.7 4.5 %fusion.6 = f32[2,128,256]{2,1,0:T(8,128)S(1)} fusion(bf16[2,2,256,4096]{3,2,1,0:T(8,128)(2,1)} %param.4, bf16[2,2,128,4096]{3,2,1,0:T(8,128)(2,1)} %all-gather.2.cloned.1.call-done), kind=kOutput, calls=%fused_computation.9 | convolution fusion | flops 536870912 | bytes 6553600 | tf_op jit(solution)/shard_map/fps,frs->fpr/dot_general | solution.py:37
  125.3 1.5 fusion.45
  126.8 1.5 fusion.42
  128.4 1.0 copy.12
  129.4 8.4 %all-to-all-start = ((bf16[2,2,128,256]{3,1,0,2:T(2,128)(2,1)}), bf16[2,2,128,256]{3,1,0,2:T(2,128)(2,1)S(1)}, u32[]{:S(2)}, u32[]{:S(2)}) async-start(bf16[2,2,128,256]{3,1,0,2:T(2,128)(2,1)} %copy.12), calls=%async_computation | async-start | bytes 524288 | tf_op jit(solution)/shard_map/all_to_all | solution.py:41
  137.8 0.7 dynamic-slice_bitcast_fusion
  138.5 6.6 %all-to-all-done = bf16[2,2,128,256]{3,1,0,2:T(2,128)(2,1)S(1)} async-done(((bf16[2,2,128,256]{3,1,0,2:T(2,128)(2,1)}), bf16[2,2,128,256]{3,1,0,2:T(2,128)(2,1)S(1)}, u32[]{:S(2)}, u32[]{:S(2)}) %all-to-all-start) | async-done | bytes 262176 | tf_op jit(solution)/shard_map/all_to_all | solution.py:41
  145.8 0.6 fusion.25
  147.7 10.3 %all_to_all.57 = bf16[2,32,8,256]{3,2,0,1:T(8,128)(2,1)S(1)} all-to-all(bf16[2,32,8,256]{3,2,0,1:T(8,128)(2,1)S(1)} %pad_maximum_fusion.2), channel_id=1, replica_groups=mesh['freq'=16,'rcv'=16] {'freq'}, dimensions={1} | all-to-all | bytes 524288 | tf_op jit(solution)/shard_map/all_to_all | solution.py:45
  158.0 3.1 fusion.10
  161.6 0.7 fusion.8
  162.3 0.8 fusion.1
  163.1 0.8 fusion
  163.9 3.8 pad_maximum_fusion
  167.7 217.9 %reduce-scatter.2.cloned.1.call-done = f32[256,2,2,128]{0,3,2,1:T(8,128)} async-done(((f32[4096,2,2,128]{0,3,2,1:T(8,128)}), f32[256,2,2,128]{0,3,2,1:T(8,128)}) %reduce-scatter.2.cloned.1.call-update) | async-done | bytes 524304 | tf_op jit(solution)/shard_map/reduce_scatter | solution.py:70
  385.6 1.1 convert_bitcast_fusion.1
  386.9 16.4 %all_to_all.58 = bf16[2,2,128,256]{3,1,0,2:T(2,128)(2,1)S(1)} all-to-all(bf16[2,2,128,256]{3,1,0,2:T(2,128)(2,1)S(1)} %copy.17), channel_id=1, replica_groups=mesh['freq'=16,'rcv'=16] {'freq'}, dimensions={2} | all-to-all | bytes 524288 | tf_op jit(solution)/shard_map/all_to_all | solution.py:41
  404.0 0.6 fusion.27
  404.6 0.6 fusion.29
  405.9 10.3 %all_to_all.59 = bf16[2,32,8,256]{3,2,0,1:T(8,128)(2,1)S(1)} all-to-all(bf16[2,32,8,256]{3,2,0,1:T(8,128)(2,1)S(1)} %pad_maximum_fusion.3), channel_id=1, replica_groups=mesh['freq'=16,'rcv'=16] {'freq'}, dimensions={1} | all-to-all | bytes 524288 | tf_op jit(solution)/shard_map/all_to_all | solution.py:45
  416.2 0.8 fusion.48
  (46 shorter events, 3.9 us)
Async XLA Ops:
  7.2 109.0 %all-gather.2.cloned.1.call-start = ((), (), s32[]{:S(2)}) async-start(), calls=%async_computation.5 | async-start | bytes 4456448 | tf_op jit(solution)/shard_map/all_gather | solution.py:53
  116.2 9.0 %slice-start = ((s8[8388608]{0:T(1024)(128)(4,1)}), s8[4194304]{0:T(1024)(128)(4,1)S(1)}, s32[]{:S(2)}) async-start(s8[8388608]{0:T(1024)(128)(4,1)} %bitcast.149), calls=%async_computation.7 | async-start | bytes 8388608
  116.2 9.0 %copy-start.2 = (bf16[2,2,128,4096]{3,2,1,0:T(8,128)(2,1)S(1)}, bf16[2,2,128,4096]{3,2,1,0:T(8,128)(2,1)}, u32[]{:S(2)}) copy-start(bf16[2,2,128,4096]{3,2,1,0:T(8,128)(2,1)} %all-gather.2.cloned.1.call-done) | copy-start | bytes 12582916
  120.7 4.5 %slice-start.1 = ((s8[8388608]{0:T(1024)(128)(4,1)}), s8[4194304]{0:T(1024)(128)(4,1)S(1)}, s32[]{:S(2)}) async-start(s8[8388608]{0:T(1024)(128)(4,1)} %bitcast.149), calls=%async_computation.8 | async-start | bytes 8388608
  129.4 15.8 %all-to-all-start = ((bf16[2,2,128,256]{3,1,0,2:T(2,128)(2,1)}), bf16[2,2,128,256]{3,1,0,2:T(2,128)(2,1)S(1)}, u32[]{:S(2)}, u32[]{:S(2)}) async-start(bf16[2,2,128,256]{3,1,0,2:T(2,128)(2,1)} %copy.12), calls=%async_computation | async-start | bytes 524288 | tf_op jit(solution)/shard_map/all_to_all | solution.py:41
  137.8 247.8 %reduce-scatter.2.cloned.1.call-start = ((), (), s32[]{:S(2)}) async-start(), calls=%async_computation.6 | async-start | bytes 8912896 | tf_op jit(solution)/shard_map/reduce_scatter | solution.py:70
  145.2 15.9 %slice-start.2 = ((s8[8388608]{0:T(1024)(128)(4,1)}), s8[4194304]{0:T(1024)(128)(4,1)S(1)}, s32[]{:S(2)}) async-start(s8[8388608]{0:T(1024)(128)(4,1)} %bitcast.151), calls=%async_computation.9 | async-start | bytes 8388608
  158.0 5.1 %copy-start = (bf16[2,16,2,8,256]{4,3,1,2,0:T(8,128)(2,1)}, bf16[2,16,2,8,256]{4,3,1,2,0:T(8,128)(2,1)S(1)}, u32[]{:S(2)}) copy-start(bf16[2,16,2,8,256]{4,3,1,2,0:T(8,128)(2,1)S(1)} %copy.39) | copy-start | bytes 786436
  158.0 3.5 slice-start.3
  167.7 248.5 %copy-start.1 = (bf16[2,2,128,256]{3,2,1,0:T(8,128)(2,1)S(1)}, bf16[2,2,128,256]{3,2,1,0:T(8,128)(2,1)}, u32[]{:S(2)}) copy-start(bf16[2,2,128,256]{3,2,1,0:T(8,128)(2,1)} %param.6) | copy-start | bytes 786436
Sparse Core Ops, SparseCore 0:
  10.5 105.6 all-gather.1
  167.8 217.7 reduce-scatter.1
where the time goes:
time: 424 us
  waiting for transfers between devices  334 us (79%)
  blocking collectives  37 us (9%)
  matrix products  21.9 us (5%)
  between operations  14.4 us (3%)
  starting transfers between devices  8.46 us (2%)
  other arithmetic  6.4 us (2%)
    reduce_scatter x1, waiting for transfers between devices, local(): lax.psum_scatter(jnp.stack([real_term, imag_term], axis=1), 'rcv', scatte...  218 us
    all_gather x1, waiting for transfers between devices, local(): segment = lax.all_gather(focus_plus, 'rcv', axis=3, tiled=True)  108 us
    all_to_all x2, blocking collectives, time_window(): lax.all_to_all(windowed(shuffled, local_arrival), 'freq', split_axis=1, c...  20.6 us
    dot_general x8, matrix products, product(): return jnp.einsum(pattern, left, right, preferred_element_type=jnp.float32)  17.4 us
    all_to_all x1, blocking collectives, time_window(): lax.all_to_all(spectrum, 'freq', split_axis=2, concat_axis=1, tiled=True)  16.4 us
  transfers between devices with their start and end apart: 3, of which 3 were waited for; matrix products, arithmetic and copies ran while one was open for 0% of the time, Pallas kernels for 0%

commit v1 on v0

v1 whole, which is shorter than its diff:
```python
import functools

import jax
import jax.numpy as jnp
import ml_dtypes
import numpy as np
from jax import lax
from jax.experimental import pallas as pl
from jax.experimental.pallas import tpu as pltpu
from jax.sharding import PartitionSpec as P

MESH = pl.DeviceIdType.MESH
BF = jnp.bfloat16
F32 = jnp.float32

FOCAL = 128
BLOCK = 256
POSITIONS = 4096
GROUP = 16
RING = 8
SAMPLES = 64
CHUNKS = 2
PC = FOCAL // CHUNKS
PG = PC // 8
NH = GROUP // PG
W = BLOCK // NH
ROWS = 8 * SAMPLES

ARRIVALS = (
    ((0, 1), "f"),
    ((0, -1), "by"),
    ((1, 0), "f"),
    ((0, 2), "fy"),
    ((0, -2), "by"),
    ((1, -1), ""),
    ((1, 1), ""),
    ((0, 3), "f"),
    ((0, -3), ""),
    ((1, 2), "f"),
    ((1, -2), "b"),
    ((0, 4), "y"),
    ((1, 3), ""),
    ((1, -3), ""),
    ((1, 4), ""),
)
SLOT = {where: number for number, (where, _) in enumerate(ARRIVALS)}


def after(where, send):
    column, distance = where
    if send == "y":
        return (1 - column, distance)
    return (column, distance + (1 if send == "f" else -1))


def split(table):
    high = table.astype(ml_dtypes.bfloat16)
    low = (table - high.astype(np.float64)).astype(ml_dtypes.bfloat16)
    return np.stack([high, low])


def transforms():
    sample = np.arange(SAMPLES)
    frequency = np.arange(SAMPLES // 2)
    angle = 2.0 * np.pi * ((sample[:, None] * frequency[None, :]) % SAMPLES) / SAMPLES
    table = np.stack([np.cos(angle), -np.sin(angle)], 1).reshape(SAMPLES, 2, GROUP, 2).transpose(0, 2, 1, 3)
    table = table.reshape(SAMPLES, SAMPLES)
    eye = np.eye(8)
    forth = np.kron(table / (SAMPLES // 2), eye)
    back = np.kron(table.T, eye)
    return split(forth), split(back)


def dot(left, right):
    return lax.dot_general(left, right, (((1,), (0,)), ((), ())), preferred_element_type=F32)


def dot_t(left, right):
    return lax.dot_general(left, right, (((1,), (1,)), ((), ())), preferred_element_type=F32)


def kernel(
    refl_hbm, plus_hbm, direct_hbm, arrival_hbm, forth_hbm, back_hbm,
    minus_hbm, next_hbm,
    refl, direct, arrival, forth, back, gathered, send_up, got_up, send_back, got_back, masked, result,
    load_sems, plus_sems, out_sems, gather_recv, gather_send, swap_recv, swap_send,
):
    me_f = lax.axis_index("freq")
    me_r = lax.axis_index("rcv")
    core = lax.rem(me_f, 2)
    z = lax.div(me_r, 2)
    high = lax.rem(me_r, 2)
    turn = 1 - 2 * core

    def place(column, distance):
        ring = lax.rem(z - turn * distance + 2 * RING, RING)
        return ring * 2 + (high if column == 0 else 1 - high)

    targets = {
        "f": (me_f, place(0, -1)),
        "b": (me_f, place(0, 1)),
        "y": (me_f, place(1, 0)),
    }

    loads = [
        pltpu.make_async_copy(source, target, load_sems.at[number])
        for number, (source, target) in enumerate(
            ((refl_hbm, refl), (direct_hbm, direct), (arrival_hbm, arrival), (forth_hbm, forth), (back_hbm, back))
        )
    ]

    def block_of(job, where):
        start = pl.multiple_of(place(*where) * BLOCK, BLOCK)
        return gathered.at[job, :, :, :, pl.ds(start, BLOCK)]

    own = [
        pltpu.make_async_copy(
            plus_hbm.at[:, :, pl.ds(chunk * PC, PC), :], block_of(chunk, (0, 0)), plus_sems.at[chunk]
        )
        for chunk in range(CHUNKS)
    ]
    for copy in own:
        copy.start()
    for copy in loads:
        copy.start()

    barrier = pltpu.get_barrier_semaphore()
    for target in targets.values():
        pl.semaphore_signal(barrier, inc=1, device_id=target, device_id_type=MESH)

    @pl.loop(1, GROUP)
    def _(step):
        pl.semaphore_signal(
            barrier, inc=1, device_id=(lax.rem(me_f + step, GROUP), me_r), device_id_type=MESH
        )

    pl.semaphore_wait(barrier, 3 + GROUP - 1)

    def gather_copy(job, where, send):
        block = block_of(job, where)
        return pltpu.make_async_remote_copy(
            src_ref=block,
            dst_ref=block,
            send_sem=gather_send.at[job],
            recv_sem=gather_recv.at[job, SLOT[after(where, send)]],
            device_id=targets[send],
            device_id_type=MESH,
        )

    def gather_start(job):
        for send in "fby":
            gather_copy(job, (0, 0), send).start()

    def gather_step(job, number):
        where, sends = ARRIVALS[number]
        block = block_of(job, where)
        pltpu.make_async_remote_copy(
            src_ref=block,
            dst_ref=block,
            send_sem=gather_send.at[job],
            recv_sem=gather_recv.at[job, number],
            device_id=targets["f"],
            device_id_type=MESH,
        ).wait_recv()
        for send in sends:
            gather_copy(job, where, send).start()

    def gather_end(job):
        sent = gathered.at[job, :, :, :, pl.ds(0, (GROUP - 1) * BLOCK)]
        pltpu.make_async_remote_copy(
            src_ref=sent,
            dst_ref=sent,
            send_sem=gather_send.at[job],
            recv_sem=gather_recv.at[job, 0],
            device_id=targets["f"],
            device_id_type=MESH,
        ).wait_send()

    def products(job):
        sums = []
        for freq in range(2):
            left = gathered[job, :, freq].reshape(2 * PC, POSITIONS)
            with_real = dot_t(left, refl[0, freq])
            with_imag = dot_t(left, refl[1, freq])
            if job < CHUNKS:
                sums.append((with_real[:PC] - with_imag[PC:], with_real[PC:] + with_imag[:PC]))
            else:
                sums.append((with_real[:PC] + with_imag[PC:], with_real[PC:] - with_imag[:PC]))
        for comp in range(2):
            pair = [sums[freq][comp].reshape(PG, 8, BLOCK) for freq in range(2)]
            pair = jnp.concatenate(pair, axis=1).astype(BF)
            for part in range(NH):
                send_up[job, pl.ds(part * PG, PG), pl.ds(comp * 16, 16), :] = pair[:, :, part * W:(part + 1) * W]

    def swap_copy(job, way, sent, got, owner, count=1):
        if count == 1:
            source, target = sent.at[job, owner], got.at[job, me_f]
        else:
            source, target = sent.at[job, pl.ds(0, count)], got.at[job, pl.ds(0, count)]
        return pltpu.make_async_remote_copy(
            src_ref=source,
            dst_ref=target,
            send_sem=swap_send.at[job, way],
            recv_sem=swap_recv.at[job, way],
            device_id=(owner, me_r),
            device_id_type=MESH,
        )

    def swap_start(job, way, sent, got):
        @pl.loop(1, GROUP)
        def _(step):
            swap_copy(job, way, sent, got, lax.rem(me_f + step, GROUP)).start()

        got[job, me_f] = sent[job, me_f]

    def swap_wait(job, way, sent, got):
        other = lax.rem(me_f + 1, GROUP)
        swap_copy(job, way, sent, got, other, GROUP - 1).wait_recv()

    def swap_end(job, way, sent, got):
        other = lax.rem(me_f + 1, GROUP)
        swap_copy(job, way, sent, got, other, GROUP - 1).wait_send()

    def window(job):
        chunk = job % CHUNKS
        first = pl.multiple_of(chunk * PC + lax.rem(me_f, PG) * 8, 8)
        column = pl.multiple_of(lax.div(me_f, PG) * W, W)
        times = arrival[pl.ds(first, 8), pl.ds(column, W)][None]
        spectra = got_up[job].reshape(ROWS, W)
        for part in range(4):
            rows = ROWS // 4
            here = pl.ds(part * rows, rows)
            traces = dot(forth[0, here], spectra) + dot(forth[1, here], spectra)
            sample = lax.broadcasted_iota(jnp.int32, (rows // 8, 8, W), 0) + part * (rows // 8)
            inside = (sample < times) | (sample > SAMPLES - times)
            kept = jnp.where(inside, traces.reshape(rows // 8, 8, W), 0.0).reshape(rows, W)
            upper = kept.astype(BF)
            masked[0, here] = upper
            masked[1, here] = (kept - upper.astype(F32)).astype(BF)
        for part in range(4):
            here = pl.ds(part * rows, rows)
            spectrum = dot(back[0, here], masked[0]) + dot(back[1, here], masked[0]) + dot(back[0, here], masked[1])
            send_back[job, pl.ds(part * 4, 4)] = spectrum.astype(BF).reshape(4, 32, W)

    def returned(job, comp):
        value = got_back[job, :, pl.ds(comp * 16, 16), :].astype(F32)
        parts = []
        for freq in range(2):
            one = value[:, freq * 8:(freq + 1) * 8, :].reshape(NH, PC, W)
            parts.append(jnp.concatenate([one[part] for part in range(NH)], axis=1))
        return parts

    def place_minus(job):
        chunk = job % CHUNKS
        start = pl.multiple_of(me_r * BLOCK, BLOCK)
        for comp in range(2):
            for freq, value in enumerate(returned(job, comp)):
                gathered[CHUNKS + chunk, comp, freq, :, pl.ds(start, BLOCK)] = value.astype(BF)
        minus_copy(chunk).start()

    def minus_copy(chunk):
        return pltpu.make_async_copy(
            block_of(CHUNKS + chunk, (0, 0)), minus_hbm.at[:, :, pl.ds(chunk * PC, PC), :], out_sems.at[chunk]
        )

    def next_copy(chunk):
        here = pl.ds(chunk * PC, PC)
        return pltpu.make_async_copy(
            result.at[:, :, here, :], next_hbm.at[:, :, here, :], out_sems.at[CHUNKS + chunk]
        )

    def place_next(job):
        chunk = job % CHUNKS
        here = pl.ds(chunk * PC, PC)
        for comp in range(2):
            for freq, value in enumerate(returned(job, comp)):
                value = value.astype(BF).astype(F32)
                result[comp, freq, here, :] = (direct[comp, freq, here, :].astype(F32) + value).astype(BF)
        next_copy(chunk).start()

    steps = []

    def plan(job, begin):
        for number in range(len(ARRIVALS)):
            when = begin + STEP_TIMES[number]
            steps.append((when, functools.partial(gather_step, job, number)))

    STEP_TIMES = (3.5, 3.6, 3.7, 7.0, 7.1, 7.2, 7.3, 10.5, 10.6, 10.7, 10.8, 13.0, 13.5, 13.6, 15.0)

    def tail(job, begin):
        steps.append((begin, functools.partial(products, job)))
        steps.append((begin + 2.0, functools.partial(swap_start, job, 0, send_up, got_up)))
        steps.append((begin + 6.5, functools.partial(swap_wait, job, 0, send_up, got_up)))
        steps.append((begin + 6.6, functools.partial(window, job)))
        steps.append((begin + 8.0, functools.partial(swap_start, job, 1, send_back, got_back)))
        steps.append((begin + 12.0, functools.partial(swap_wait, job, 1, send_back, got_back)))
        steps.append((begin + 12.1, functools.partial(place_minus if job < CHUNKS else place_next, job)))

    def first_products():
        loads[0].wait()

    def first_window():
        for copy in loads[2:]:
            copy.wait()

    START = (0.0, 7.0, 29.0, 42.0) if CHUNKS == 2 else (0.0, 40.0)
    LENGTH = 16.0
    for job in range(2 * CHUNKS):
        begin = START[job]
        if job < CHUNKS:
            steps.append((begin - 0.1, own[job].wait))
        steps.append((begin, functools.partial(gather_start, job)))
        plan(job, begin)
        end = begin + LENGTH + (5.0 if job == 1 else 0.0)
        if job == 0:
            steps.append((end - 0.1, first_products))
            steps.append((end + 6.55, first_window))
        if job == CHUNKS:
            steps.append((end - 0.1, loads[1].wait))
        tail(job, end)
    for _, step in sorted(steps, key=lambda entry: entry[0]):
        step()

    for job in range(2 * CHUNKS):
        gather_end(job)
        swap_end(job, 0, send_up, got_up)
        swap_end(job, 1, send_back, got_back)
    for chunk in range(CHUNKS):
        minus_copy(chunk).wait()
        next_copy(chunk).wait()


def local(reflection, focus_plus, focus_direct, arrival):
    forth, back = transforms()
    jobs = 2 * CHUNKS
    swap = (jobs, GROUP, 32, W)
    anywhere = pl.BlockSpec(memory_space=pl.ANY)
    output = jax.ShapeDtypeStruct(focus_plus.shape, BF)
    return pl.pallas_call(
        kernel,
        out_shape=(output, output),
        in_specs=[anywhere] * 6,
        out_specs=(anywhere, anywhere),
        scratch_shapes=[
            pltpu.VMEM(reflection.shape, BF),
            pltpu.VMEM(focus_direct.shape, BF),
            pltpu.VMEM(arrival.shape, jnp.int32),
            pltpu.VMEM(forth.shape, BF),
            pltpu.VMEM(back.shape, BF),
            pltpu.VMEM((jobs, 2, 2, PC, POSITIONS), BF),
            pltpu.VMEM(swap, BF),
            pltpu.VMEM(swap, BF),
            pltpu.VMEM(swap, BF),
            pltpu.VMEM(swap, BF),
            pltpu.VMEM((2, ROWS, W), BF),
            pltpu.VMEM(focus_direct.shape, BF),
            pltpu.SemaphoreType.DMA((5,)),
            pltpu.SemaphoreType.DMA((CHUNKS,)),
            pltpu.SemaphoreType.DMA((2 * CHUNKS,)),
            pltpu.SemaphoreType.DMA((jobs, len(ARRIVALS))),
            pltpu.SemaphoreType.DMA((jobs,)),
            pltpu.SemaphoreType.DMA((jobs, 2)),
            pltpu.SemaphoreType.DMA((jobs, 2)),
        ],
        compiler_params=pltpu.CompilerParams(
            collective_id=0, has_side_effects=True, vmem_limit_bytes=48 * 2**20
        ),
    )(reflection, focus_plus, focus_direct, arrival, jnp.asarray(forth), jnp.asarray(back))


def solution(mesh):
    return jax.shard_map(
        local,
        mesh=mesh,
        in_specs=(
            P(None, "freq", "rcv", None),
            P(None, "freq", None, "rcv"),
            P(None, "freq", None, "rcv"),
            P(None, "rcv"),
        ),
        out_specs=(P(None, "freq", None, "rcv"), P(None, "freq", None, "rcv")),
        check_vma=False,
    )
```

time: 424 us -> 124 us (0.29)
  waiting for transfers between devices: 334 us -> 0 us
  Pallas kernels: 0 us -> 117 us
  blocking collectives: 37 us -> 0 us
  matrix products: 21.9 us -> 0 us
  between operations: 14.4 us -> 0.65 us
  starting transfers between devices: 8.46 us -> 0 us
  other arithmetic: 6.4 us -> 0 us
  local copies, waits for them, and re-layouts: 2.12 us -> 6.65 us
    reduce_scatter x1 -> x0, waiting for transfers between devices: 218 us -> none  [local(): lax.psum_scatter(jnp.stack([real_term, imag_term], axis=1), 'rcv', scatte...]
    pallas_call x0 -> x1, Pallas kernels: none -> 117 us  [local(): pl.pallas_call(kernel, out_shape=(output, output), in_specs=[anywhere] *...]
    all_gather x1 -> x0, waiting for transfers between devices: 108 us -> none  [local(): segment = lax.all_gather(focus_plus, 'rcv', axis=3, tiled=True)]
    all_to_all x3 -> x0, blocking collectives: 37 us -> none  [the longest x2 20.6 us: time_window(): lax.all_to_all(windowed(shuffled, local_arrival), 'freq', split_axis=1, c...]
    dot_general x16 -> x0, matrix products: 21.9 us -> none  [the longest x8 17.4 us: product(): return jnp.einsum(pattern, left, right, preferred_element_type=jnp.float32)]
    all_to_all x1 -> x0, starting transfers between devices: 8.39 us -> none  [time_window(): lax.all_to_all(spectrum, 'freq', split_axis=2, concat_axis=1, tiled=True)]
    all_to_all x1 -> x0, waiting for transfers between devices: 6.63 us -> none  [time_window(): lax.all_to_all(spectrum, 'freq', split_axis=2, concat_axis=1, tiled=True)]
    unnamed x24 -> x12, local copies, waits for them, and re-layouts: 0.71 us -> 6.65 us
  transfers between devices with their start and end apart: 3 -> 0, of which waited for: 3 -> 0; matrix products, arithmetic and copies ran while one was open for 0% -> 0% of each run, Pallas kernels for 0% -> 0%
where the time goes in v1:
time: 124 us
  Pallas kernels  117 us (94%)
  local copies, waits for them, and re-layouts  6.65 us (5%)
    pallas_call x1, Pallas kernels, local(): pl.pallas_call(kernel, out_shape=(output, output), in_specs=[anywhere] *...  117 us
    unnamed x12, local copies, waits for them, and re-layouts  6.65 us

profile of v1, /device:TPU:1, one launch (start us, length us, event | category | flops | bytes accessed | tf_op | source)
XLA Modules:
  0.0 123.8 jit_solution(12442276100792248043)
XLA Ops:
  0.6 0.0 copy-start
  0.6 1.2 copy-done
  1.9 0.0 copy-start.1
  1.9 1.2 copy-done.1
  3.1 0.0 copy-start.2
  3.1 0.9 copy-done.2
  4.0 0.0 copy-start.3
  4.0 0.9 copy-done.3
  5.0 0.0 copy-start.4
  5.0 0.9 copy-done.4
  5.9 116.5 %shard_map.77 = (bf16[2,2,128,256]{3,2,1,0:T(8,128)(2,1)S(1)}, bf16[2,2,128,256]{3,2,1,0:T(8,128)(2,1)S(1)}) custom-call(bf16[2,2,256,4096]{3,2,1,0:T(8,128)(2,1)} %refl_hbm.1, bf16[2,2,128,256]{3,2,1,0:T(8,128)(2,1)S(1)} %copy-done.2, bf16[2,2,128,256]{3,2,1,0:T(8,128)(2,1)S(1)} %copy-done.3, s32[128,256]{1,0:T(8,128)S(1)} %copy-done.4, ...), custom_call_target="tpu_custom_call" | custom-call | tf_op jit(solution)/shard_map/pallas_call | solution.py:339
  122.4 0.7 copy.10
  123.1 0.7 copy.11
Async XLA Ops:
  0.6 1.2 copy-start
  1.9 1.2 copy-start.1
  3.1 0.9 copy-start.2
  4.0 0.9 copy-start.3
  5.0 0.9 copy-start.4

commit v2 on v1

--- a/solution.py
+++ b/solution.py
@@ -15,8 +15,8 @@
 
 FOCAL = 128
 BLOCK = 256
-POSITIONS = 4096
 GROUP = 16
+FAR_FIRST = sorted(range(1, GROUP), key=lambda step: -min(step, GROUP - step))
 RING = 8
 SAMPLES = 64
 CHUNKS = 2
@@ -24,26 +24,28 @@
 PG = PC // 8
 NH = GROUP // PG
 W = BLOCK // NH
+BEGIN = (0.0, 2.3, 32.5, 34.8)
 ROWS = 8 * SAMPLES
 
 ARRIVALS = (
-    ((0, 1), "f"),
-    ((0, -1), "by"),
-    ((1, 0), "f"),
-    ((0, 2), "fy"),
-    ((0, -2), "by"),
-    ((1, -1), ""),
-    ((1, 1), ""),
-    ((0, 3), "f"),
-    ((0, -3), ""),
-    ((1, 2), "f"),
-    ((1, -2), "b"),
-    ((0, 4), "y"),
-    ((1, 3), ""),
-    ((1, -3), ""),
-    ((1, 4), ""),
+    ((0, 1), "fy", 3.0),
+    ((0, -1), "by", 3.4),
+    ((1, 0), "", 3.6),
+    ((0, -2), "by", 7.6),
+    ((0, 2), "f", 8.2),
+    ((1, 1), "f", 10.4),
+    ((1, -1), "", 11.0),
+    ((0, -3), "", 12.0),
+    ((0, 3), "f", 12.7),
+    ((1, 2), "f", 15.6),
+    ((0, 4), "y", 17.0),
+    ((1, -2), "b", 17.6),
+    ((1, 3), "", 19.6),
+    ((1, 4), "", 22.3),
+    ((1, -3), "", 22.5),
 )
-SLOT = {where: number for number, (where, _) in enumerate(ARRIVALS)}
+END = 22.7
+SLOT = {where: number for number, (where, _, _) in enumerate(ARRIVALS)}
 
 
 def after(where, send):
@@ -63,7 +65,7 @@
     sample = np.arange(SAMPLES)
     frequency = np.arange(SAMPLES // 2)
     angle = 2.0 * np.pi * ((sample[:, None] * frequency[None, :]) % SAMPLES) / SAMPLES
-    table = np.stack([np.cos(angle), -np.sin(angle)], 1).reshape(SAMPLES, 2, GROUP, 2).transpose(0, 2, 1, 3)
+    table = np.stack([np.cos(angle), -np.sin(angle)], 1).reshape(SAMPLES, 2, GROUP, 2).transpose(0, 2, 3, 1)
     table = table.reshape(SAMPLES, SAMPLES)
     eye = np.eye(8)
     forth = np.kron(table / (SAMPLES // 2), eye)
@@ -82,7 +84,7 @@
 def kernel(
     refl_hbm, plus_hbm, direct_hbm, arrival_hbm, forth_hbm, back_hbm,
     minus_hbm, next_hbm,
-    refl, direct, arrival, forth, back, gathered, send_up, got_up, send_back, got_back, masked, result,
+    refl, direct, arrival, forth, back, gathered, send_up, got_up, send_back, got_back, masked, result, sums,
     load_sems, plus_sems, out_sems, gather_recv, gather_send, swap_recv, swap_send,
 ):
     me_f = lax.axis_index("freq")
@@ -110,8 +112,7 @@
     ]
 
     def block_of(job, where):
-        start = pl.multiple_of(place(*where) * BLOCK, BLOCK)
-        return gathered.at[job, :, :, :, pl.ds(start, BLOCK)]
+        return gathered.at[job, place(*where)]
 
     own = [
         pltpu.make_async_copy(
@@ -152,7 +153,7 @@
             gather_copy(job, (0, 0), send).start()
 
     def gather_step(job, number):
-        where, sends = ARRIVALS[number]
+        where, sends, _ = ARRIVALS[number]
         block = block_of(job, where)
         pltpu.make_async_remote_copy(
             src_ref=block,
@@ -166,7 +167,7 @@
             gather_copy(job, where, send).start()
 
     def gather_end(job):
-        sent = gathered.at[job, :, :, :, pl.ds(0, (GROUP - 1) * BLOCK)]
+        sent = gathered.at[job, pl.ds(0, GROUP - 1)]
         pltpu.make_async_remote_copy(
             src_ref=sent,
             dst_ref=sent,
@@ -176,21 +177,29 @@
             device_id_type=MESH,
         ).wait_send()
 
+    def accumulate(job, where):
+        owner = place(*where)
+        here = pl.ds(pl.multiple_of(owner * BLOCK, BLOCK), BLOCK)
+        for freq in range(2):
+            left = gathered[job, owner, :, freq].reshape(2 * PC, BLOCK)
+            for comp in range(2):
+                term = dot_t(left, refl[comp, freq, :, here])
+                if where == (0, 0):
+                    sums[job % CHUNKS, freq, comp] = term
+                else:
+                    sums[job % CHUNKS, freq, comp] += term
+
     def products(job):
-        sums = []
         for freq in range(2):
-            left = gathered[job, :, freq].reshape(2 * PC, POSITIONS)
-            with_real = dot_t(left, refl[0, freq])
-            with_imag = dot_t(left, refl[1, freq])
+            with_real = sums[job % CHUNKS, freq, 0]
+            with_imag = sums[job % CHUNKS, freq, 1]
             if job < CHUNKS:
-                sums.append((with_real[:PC] - with_imag[PC:], with_real[PC:] + with_imag[:PC]))
+                both = (with_real[:PC] - with_imag[PC:], with_real[PC:] + with_imag[:PC])
             else:
-                sums.append((with_real[:PC] + with_imag[PC:], with_real[PC:] - with_imag[:PC]))
-        for comp in range(2):
-            pair = [sums[freq][comp].reshape(PG, 8, BLOCK) for freq in range(2)]
-            pair = jnp.concatenate(pair, axis=1).astype(BF)
-            for part in range(NH):
-                send_up[job, pl.ds(part * PG, PG), pl.ds(comp * 16, 16), :] = pair[:, :, part * W:(part + 1) * W]
+                both = (with_real[:PC] + with_imag[PC:], with_real[PC:] - with_imag[:PC])
+            pair = jnp.concatenate([one.reshape(PG, 8, BLOCK) for one in both], axis=1).astype(BF)
+            for half in range(NH):
+                send_up[job, pl.ds(half * PG, PG), pl.ds(freq * 16, 16), :] = pair[:, :, half * W:(half + 1) * W]
 
     def swap_copy(job, way, sent, got, owner, count=1):
         if count == 1:
@@ -207,8 +216,7 @@
         )
 
     def swap_start(job, way, sent, got):
-        @pl.loop(1, GROUP)
-        def _(step):
+        for step in FAR_FIRST:
             swap_copy(job, way, sent, got, lax.rem(me_f + step, GROUP)).start()
 
         got[job, me_f] = sent[job, me_f]
@@ -242,20 +250,17 @@
             spectrum = dot(back[0, here], masked[0]) + dot(back[1, here], masked[0]) + dot(back[0, here], masked[1])
             send_back[job, pl.ds(part * 4, 4)] = spectrum.astype(BF).reshape(4, 32, W)
 
-    def returned(job, comp):
-        value = got_back[job, :, pl.ds(comp * 16, 16), :].astype(F32)
-        parts = []
+    def returned(job):
         for freq in range(2):
-            one = value[:, freq * 8:(freq + 1) * 8, :].reshape(NH, PC, W)
-            parts.append(jnp.concatenate([one[part] for part in range(NH)], axis=1))
-        return parts
+            value = got_back[job, :, pl.ds(freq * 16, 16), :].astype(F32)
+            for comp in range(2):
+                one = value[:, comp * 8:(comp + 1) * 8, :].reshape(NH, PC, W)
+                yield comp, freq, jnp.concatenate([one[half] for half in range(NH)], axis=1)
 
     def place_minus(job):
         chunk = job % CHUNKS
-        start = pl.multiple_of(me_r * BLOCK, BLOCK)
-        for comp in range(2):
-            for freq, value in enumerate(returned(job, comp)):
-                gathered[CHUNKS + chunk, comp, freq, :, pl.ds(start, BLOCK)] = value.astype(BF)
+        for comp, freq, value in returned(job):
+            gathered[CHUNKS + chunk, me_r, comp, freq] = value.astype(BF)
         minus_copy(chunk).start()
 
     def minus_copy(chunk):
@@ -272,52 +277,42 @@
     def place_next(job):
         chunk = job % CHUNKS
         here = pl.ds(chunk * PC, PC)
-        for comp in range(2):
-            for freq, value in enumerate(returned(job, comp)):
-                value = value.astype(BF).astype(F32)
-                result[comp, freq, here, :] = (direct[comp, freq, here, :].astype(F32) + value).astype(BF)
+        for comp, freq, value in returned(job):
+            value = value.astype(BF).astype(F32)
+            result[comp, freq, here, :] = (direct[comp, freq, here, :].astype(F32) + value).astype(BF)
         next_copy(chunk).start()
 
     steps = []
 
-    def plan(job, begin):
-        for number in range(len(ARRIVALS)):
-            when = begin + STEP_TIMES[number]
-            steps.append((when, functools.partial(gather_step, job, number)))
-
-    STEP_TIMES = (3.5, 3.6, 3.7, 7.0, 7.1, 7.2, 7.3, 10.5, 10.6, 10.7, 10.8, 13.0, 13.5, 13.6, 15.0)
-
-    def tail(job, begin):
-        steps.append((begin, functools.partial(products, job)))
-        steps.append((begin + 2.0, functools.partial(swap_start, job, 0, send_up, got_up)))
-        steps.append((begin + 6.5, functools.partial(swap_wait, job, 0, send_up, got_up)))
-        steps.append((begin + 6.6, functools.partial(window, job)))
-        steps.append((begin + 8.0, functools.partial(swap_start, job, 1, send_back, got_back)))
-        steps.append((begin + 12.0, functools.partial(swap_wait, job, 1, send_back, got_back)))
-        steps.append((begin + 12.1, functools.partial(place_minus if job < CHUNKS else place_next, job)))
-
-    def first_products():
-        loads[0].wait()
-
-    def first_window():
-        for copy in loads[2:]:
+    def plan(when, what, *given):
+        steps.append((when, functools.partial(what, *given)))
+
+    def wait_all(*copies):
+        for copy in copies:
             copy.wait()
 
-    START = (0.0, 7.0, 29.0, 42.0) if CHUNKS == 2 else (0.0, 40.0)
-    LENGTH = 16.0
-    for job in range(2 * CHUNKS):
-        begin = START[job]
+    for job, begin in enumerate(BEGIN):
         if job < CHUNKS:
-            steps.append((begin - 0.1, own[job].wait))
-        steps.append((begin, functools.partial(gather_start, job)))
-        plan(job, begin)
-        end = begin + LENGTH + (5.0 if job == 1 else 0.0)
+            plan(begin - 0.01, wait_all, own[job])
+        plan(begin, gather_start, job)
         if job == 0:
-            steps.append((end - 0.1, first_products))
-            steps.append((end + 6.55, first_window))
+            plan(begin + 0.5, wait_all, loads[0])
+        plan(begin + 0.6, accumulate, job, (0, 0))
+        for number, (where, _, due) in enumerate(ARRIVALS):
+            plan(begin + due, gather_step, job, number)
+            plan(begin + due + 0.05, accumulate, job, where)
+        end = begin + END
+        if job == 0:
+            plan(end + 4.0, wait_all, *loads[2:])
         if job == CHUNKS:
-            steps.append((end - 0.1, loads[1].wait))
-        tail(job, end)
+            plan(end, wait_all, loads[1])
+        plan(end, products, job)
+        plan(end + 0.1, swap_start, job, 0, send_up, got_up)
+        plan(end + 4.0, swap_wait, job, 0, send_up, got_up)
+        plan(end + 4.1, window, job)
+        plan(end + 4.2, swap_start, job, 1, send_back, got_back)
+        plan(end + 8.5, swap_wait, job, 1, send_back, got_back)
+        plan(end + 8.6, place_minus if job < CHUNKS else place_next, job)
     for _, step in sorted(steps, key=lambda entry: entry[0]):
         step()
 
@@ -330,13 +325,18 @@
         next_copy(chunk).wait()
 
 
+def hand_on(minus, following, minus_out, next_out):
+    minus_out[...] = minus[...]
+    next_out[...] = following[...]
+
+
 def local(reflection, focus_plus, focus_direct, arrival):
     forth, back = transforms()
     jobs = 2 * CHUNKS
     swap = (jobs, GROUP, 32, W)
     anywhere = pl.BlockSpec(memory_space=pl.ANY)
     output = jax.ShapeDtypeStruct(focus_plus.shape, BF)
-    return pl.pallas_call(
+    minus, following = pl.pallas_call(
         kernel,
         out_shape=(output, output),
         in_specs=[anywhere] * 6,
@@ -347,13 +347,14 @@
             pltpu.VMEM(arrival.shape, jnp.int32),
             pltpu.VMEM(forth.shape, BF),
             pltpu.VMEM(back.shape, BF),
-            pltpu.VMEM((jobs, 2, 2, PC, POSITIONS), BF),
+            pltpu.VMEM((jobs, GROUP, 2, 2, PC, BLOCK), BF),
             pltpu.VMEM(swap, BF),
             pltpu.VMEM(swap, BF),
             pltpu.VMEM(swap, BF),
             pltpu.VMEM(swap, BF),
             pltpu.VMEM((2, ROWS, W), BF),
             pltpu.VMEM(focus_direct.shape, BF),
+            pltpu.VMEM((CHUNKS, 2, 2, 2 * PC, BLOCK), F32),
             pltpu.SemaphoreType.DMA((5,)),
             pltpu.SemaphoreType.DMA((CHUNKS,)),
             pltpu.SemaphoreType.DMA((2 * CHUNKS,)),
@@ -363,9 +364,15 @@
             pltpu.SemaphoreType.DMA((jobs, 2)),
         ],
         compiler_params=pltpu.CompilerParams(
-            collective_id=0, has_side_effects=True, vmem_limit_bytes=48 * 2**20
+            collective_id=0, has_side_effects=True, vmem_limit_bytes=62 * 2**20
         ),
     )(reflection, focus_plus, focus_direct, arrival, jnp.asarray(forth), jnp.asarray(back))
+    return pl.pallas_call(
+        hand_on,
+        out_shape=(output, output),
+        in_specs=[pl.BlockSpec(memory_space=pltpu.VMEM)] * 2,
+        out_specs=(pl.BlockSpec(memory_space=pltpu.VMEM),) * 2,
+    )(minus, following)
 
 
 def solution(mesh):

time: 124 us -> 98.1 us (0.79)
  Pallas kernels: 117 us -> 97.4 us
  local copies, waits for them, and re-layouts: 6.65 us -> 0 us
    pallas_call x1, Pallas kernels: 117 us -> 95.6 us  [local(): pl.pallas_call(kernel, out_shape=(output, output), in_specs=[anywhere] *...]
    unnamed x12 -> x0, local copies, waits for them, and re-layouts: 6.65 us -> none
    pallas_call x0 -> x1, Pallas kernels: none -> 1.84 us  [local(): pl.pallas_call(hand_on, out_shape=(output, output), in_specs=[pl.BlockSpe...]
where the time goes in v2:
time: 98.1 us; the launch traced here: 98 us
  Pallas kernels  97.4 us (99%)
    pallas_call x1, Pallas kernels, local(): pl.pallas_call(kernel, out_shape=(output, output), in_specs=[anywhere] *...  95.6 us

profile of v2, /device:TPU:1, one launch (start us, length us, event | category | flops | bytes accessed | tf_op | source)
XLA Modules:
  0.0 98.0 jit_solution(18110006997710317393)
XLA Ops:
  0.6 95.6 %shard_map.77 = (bf16[2,2,128,256]{3,2,1,0:T(8,128)(2,1)}, bf16[2,2,128,256]{3,2,1,0:T(8,128)(2,1)}) custom-call(bf16[2,2,256,4096]{3,2,1,0:T(8,128)(2,1)} %refl_hbm.1, bf16[2,2,128,256]{3,2,1,0:T(8,128)(2,1)} %plus_hbm.1, bf16[2,2,128,256]{3,2,1,0:T(8,128)(2,1)} %direct_hbm.1, s32[128,256]{1,0:T(8,128)} %arrival_hbm.1, ...), custom_call_target="tpu_custom_call" | custom-call | tf_op jit(solution)/shard_map/pallas_call | solution.py:339
  96.2 1.8 %shard_map.78 = (bf16[2,2,128,256]{3,2,1,0:T(8,128)(2,1)}, bf16[2,2,128,256]{3,2,1,0:T(8,128)(2,1)}) custom-call(bf16[2,2,128,256]{3,2,1,0:T(8,128)(2,1)} %get-tuple-element.4.minus, bf16[2,2,128,256]{3,2,1,0:T(8,128)(2,1)} %get-tuple-element.5.following), custom_call_target="tpu_custom_call" | custom-call | tf_op jit(solution)/shard_map/pallas_call | solution.py:370

commit v3 on v2

--- a/solution.py
+++ b/solution.py
@@ -22,24 +22,22 @@
 CHUNKS = 2
 PC = FOCAL // CHUNKS
 PG = PC // 8
-NH = GROUP // PG
-W = BLOCK // NH
 BEGIN = (0.0, 2.3, 32.5, 34.8)
-ROWS = 8 * SAMPLES
+ROWS = 8 * SAMPLES // 2
 
 ARRIVALS = (
-    ((0, 1), "fy", 3.0),
-    ((0, -1), "by", 3.4),
-    ((1, 0), "", 3.6),
-    ((0, -2), "by", 7.6),
-    ((0, 2), "f", 8.2),
-    ((1, 1), "f", 10.4),
-    ((1, -1), "", 11.0),
-    ((0, -3), "", 12.0),
-    ((0, 3), "f", 12.7),
-    ((1, 2), "f", 15.6),
-    ((0, 4), "y", 17.0),
-    ((1, -2), "b", 17.6),
+    ((0, 1), "fy", 2.6),
+    ((0, -1), "by", 2.7),
+    ((1, 0), "", 2.8),
+    ((0, 2), "f", 7.6),
+    ((0, -2), "by", 7.7),
+    ((1, 1), "f", 9.4),
+    ((0, 3), "f", 12.5),
+    ((1, -1), "", 12.6),
+    ((1, 2), "f", 15.2),
+    ((0, 4), "y", 16.5),
+    ((1, -2), "b", 17.0),
+    ((0, -3), "", 17.1),
     ((1, 3), "", 19.6),
     ((1, 4), "", 22.3),
     ((1, -3), "", 22.5),
@@ -62,14 +60,13 @@
 
 
 def transforms():
-    sample = np.arange(SAMPLES)
-    frequency = np.arange(SAMPLES // 2)
-    angle = 2.0 * np.pi * ((sample[:, None] * frequency[None, :]) % SAMPLES) / SAMPLES
-    table = np.stack([np.cos(angle), -np.sin(angle)], 1).reshape(SAMPLES, 2, GROUP, 2).transpose(0, 2, 3, 1)
-    table = table.reshape(SAMPLES, SAMPLES)
+    sample = np.arange(SAMPLES // 2)
+    angle = 2.0 * np.pi * ((sample[:, None] * sample[None, :]) % SAMPLES) / SAMPLES
+    weight = np.where(sample == 0, 1.0, 2.0)[:, None]
+    tables = (np.cos(angle), np.sin(angle))
     eye = np.eye(8)
-    forth = np.kron(table / (SAMPLES // 2), eye)
-    back = np.kron(table.T, eye)
+    forth = np.stack([np.kron(table / (SAMPLES // 2), eye) for table in tables])
+    back = np.stack([np.kron((weight * table).T, eye) for table in tables])
     return split(forth), split(back)
 
 
@@ -83,9 +80,9 @@
 
 def kernel(
     refl_hbm, plus_hbm, direct_hbm, arrival_hbm, forth_hbm, back_hbm,
-    minus_hbm, next_hbm,
-    refl, direct, arrival, forth, back, gathered, send_up, got_up, send_back, got_back, masked, result, sums,
-    load_sems, plus_sems, out_sems, gather_recv, gather_send, swap_recv, swap_send,
+    minus, following,
+    refl, direct, arrival, forth, back, gathered, send_up, got_up, send_back, got_back, sums,
+    load_sems, plus_sems, gather_recv, gather_send, swap_recv, swap_send,
 ):
     me_f = lax.axis_index("freq")
     me_r = lax.axis_index("rcv")
@@ -190,6 +187,7 @@
                     sums[job % CHUNKS, freq, comp] += term
 
     def products(job):
+        parts = ([], [])
         for freq in range(2):
             with_real = sums[job % CHUNKS, freq, 0]
             with_imag = sums[job % CHUNKS, freq, 1]
@@ -197,9 +195,10 @@
                 both = (with_real[:PC] - with_imag[PC:], with_real[PC:] + with_imag[:PC])
             else:
                 both = (with_real[:PC] + with_imag[PC:], with_real[PC:] - with_imag[:PC])
-            pair = jnp.concatenate([one.reshape(PG, 8, BLOCK) for one in both], axis=1).astype(BF)
-            for half in range(NH):
-                send_up[job, pl.ds(half * PG, PG), pl.ds(freq * 16, 16), :] = pair[:, :, half * W:(half + 1) * W]
+            for comp in range(2):
+                parts[comp].append(both[comp].reshape(PG, 8, BLOCK))
+        for comp in range(2):
+            send_up[job, pl.ds(comp * PG, PG)] = jnp.concatenate(parts[comp], axis=1).astype(BF)
 
     def swap_copy(job, way, sent, got, owner, count=1):
         if count == 1:
@@ -230,57 +229,37 @@
         swap_copy(job, way, sent, got, other, GROUP - 1).wait_send()
 
     def window(job):
-        chunk = job % CHUNKS
-        first = pl.multiple_of(chunk * PC + lax.rem(me_f, PG) * 8, 8)
-        column = pl.multiple_of(lax.div(me_f, PG) * W, W)
-        times = arrival[pl.ds(first, 8), pl.ds(column, W)][None]
-        spectra = got_up[job].reshape(ROWS, W)
-        for part in range(4):
-            rows = ROWS // 4
-            here = pl.ds(part * rows, rows)
-            traces = dot(forth[0, here], spectra) + dot(forth[1, here], spectra)
-            sample = lax.broadcasted_iota(jnp.int32, (rows // 8, 8, W), 0) + part * (rows // 8)
-            inside = (sample < times) | (sample > SAMPLES - times)
-            kept = jnp.where(inside, traces.reshape(rows // 8, 8, W), 0.0).reshape(rows, W)
-            upper = kept.astype(BF)
-            masked[0, here] = upper
-            masked[1, here] = (kept - upper.astype(F32)).astype(BF)
-        for part in range(4):
-            here = pl.ds(part * rows, rows)
-            spectrum = dot(back[0, here], masked[0]) + dot(back[1, here], masked[0]) + dot(back[0, here], masked[1])
-            send_back[job, pl.ds(part * 4, 4)] = spectrum.astype(BF).reshape(4, 32, W)
+        comp = lax.div(me_f, PG)
+        first = pl.multiple_of((job % CHUNKS) * PC + lax.rem(me_f, PG) * 8, 8)
+        times = arrival[pl.ds(first, 8), :][None]
+        spectra = got_up[job].reshape(ROWS, BLOCK)
+        traces = dot(forth[0, comp], spectra) + dot(forth[1, comp], spectra)
+        sample = lax.broadcasted_iota(jnp.int32, (SAMPLES // 2, 8, BLOCK), 0)
+        kept = jnp.where(sample < times, traces.reshape(SAMPLES // 2, 8, BLOCK), 0.0).reshape(ROWS, BLOCK)
+        upper = kept.astype(BF)
+        lower = (kept - upper.astype(F32)).astype(BF)
+        spectrum = dot(back[0, comp], upper) + dot(back[1, comp], upper) + dot(back[0, comp], lower)
+        send_back[job] = spectrum.astype(BF).reshape(GROUP, 16, BLOCK)
 
     def returned(job):
-        for freq in range(2):
-            value = got_back[job, :, pl.ds(freq * 16, 16), :].astype(F32)
-            for comp in range(2):
-                one = value[:, comp * 8:(comp + 1) * 8, :].reshape(NH, PC, W)
-                yield comp, freq, jnp.concatenate([one[half] for half in range(NH)], axis=1)
+        for comp in range(2):
+            value = got_back[job, pl.ds(comp * PG, PG)].astype(F32)
+            for freq in range(2):
+                yield comp, freq, value[:, freq * 8:(freq + 1) * 8].reshape(PC, BLOCK)
 
     def place_minus(job):
         chunk = job % CHUNKS
         for comp, freq, value in returned(job):
-            gathered[CHUNKS + chunk, me_r, comp, freq] = value.astype(BF)
-        minus_copy(chunk).start()
-
-    def minus_copy(chunk):
-        return pltpu.make_async_copy(
-            block_of(CHUNKS + chunk, (0, 0)), minus_hbm.at[:, :, pl.ds(chunk * PC, PC), :], out_sems.at[chunk]
-        )
-
-    def next_copy(chunk):
-        here = pl.ds(chunk * PC, PC)
-        return pltpu.make_async_copy(
-            result.at[:, :, here, :], next_hbm.at[:, :, here, :], out_sems.at[CHUNKS + chunk]
-        )
+            value = value.astype(BF)
+            gathered[CHUNKS + chunk, me_r, comp, freq] = value
+            minus[comp, freq, pl.ds(chunk * PC, PC), :] = value
 
     def place_next(job):
         chunk = job % CHUNKS
         here = pl.ds(chunk * PC, PC)
         for comp, freq, value in returned(job):
             value = value.astype(BF).astype(F32)
-            result[comp, freq, here, :] = (direct[comp, freq, here, :].astype(F32) + value).astype(BF)
-        next_copy(chunk).start()
+            following[comp, freq, here, :] = (direct[comp, freq, here, :].astype(F32) + value).astype(BF)
 
     steps = []
 
@@ -320,27 +299,18 @@
         gather_end(job)
         swap_end(job, 0, send_up, got_up)
         swap_end(job, 1, send_back, got_back)
-    for chunk in range(CHUNKS):
-        minus_copy(chunk).wait()
-        next_copy(chunk).wait()
-
-
-def hand_on(minus, following, minus_out, next_out):
-    minus_out[...] = minus[...]
-    next_out[...] = following[...]
 
 
 def local(reflection, focus_plus, focus_direct, arrival):
     forth, back = transforms()
     jobs = 2 * CHUNKS
-    swap = (jobs, GROUP, 32, W)
-    anywhere = pl.BlockSpec(memory_space=pl.ANY)
-    output = jax.ShapeDtypeStruct(focus_plus.shape, BF)
-    minus, following = pl.pallas_call(
+    swap = (jobs, GROUP, 16, BLOCK)
+    in_vmem = pl.BlockSpec(memory_space=pltpu.VMEM)
+    return pl.pallas_call(
         kernel,
-        out_shape=(output, output),
-        in_specs=[anywhere] * 6,
-        out_specs=(anywhere, anywhere),
+        out_shape=(pltpu.VMEM(focus_plus.shape, BF),) * 2,
+        in_specs=[pl.BlockSpec(memory_space=pl.ANY)] * 6,
+        out_specs=(in_vmem, in_vmem),
         scratch_shapes=[
             pltpu.VMEM(reflection.shape, BF),
             pltpu.VMEM(focus_direct.shape, BF),
@@ -352,12 +322,9 @@
             pltpu.VMEM(swap, BF),
             pltpu.VMEM(swap, BF),
             pltpu.VMEM(swap, BF),
-            pltpu.VMEM((2, ROWS, W), BF),
-            pltpu.VMEM(focus_direct.shape, BF),
             pltpu.VMEM((CHUNKS, 2, 2, 2 * PC, BLOCK), F32),
             pltpu.SemaphoreType.DMA((5,)),
             pltpu.SemaphoreType.DMA((CHUNKS,)),
-            pltpu.SemaphoreType.DMA((2 * CHUNKS,)),
             pltpu.SemaphoreType.DMA((jobs, len(ARRIVALS))),
             pltpu.SemaphoreType.DMA((jobs,)),
             pltpu.SemaphoreType.DMA((jobs, 2)),
@@ -367,12 +334,6 @@
             collective_id=0, has_side_effects=True, vmem_limit_bytes=62 * 2**20
         ),
     )(reflection, focus_plus, focus_direct, arrival, jnp.asarray(forth), jnp.asarray(back))
-    return pl.pallas_call(
-        hand_on,
-        out_shape=(output, output),
-        in_specs=[pl.BlockSpec(memory_space=pltpu.VMEM)] * 2,
-        out_specs=(pl.BlockSpec(memory_space=pltpu.VMEM),) * 2,
-    )(minus, following)
 
 
 def solution(mesh):

time: 98.1 us -> 95.8 us (0.977)
  Pallas kernels: 97.4 us -> 93.7 us
  local copies, waits for them, and re-layouts: 0 us -> 1.41 us
    pallas_call x2 -> x1, Pallas kernels: 97.4 us -> 93.7 us  [local(): pl.pallas_call(kernel, out_shape=(pltpu.VMEM(focus_plus.shape, BF),) * 2,...]
    unnamed x0 -> x2, local copies, waits for them, and re-layouts: none -> 1.41 us
where the time goes in v3:
time: 95.8 us
  Pallas kernels  93.7 us (98%)
  local copies, waits for them, and re-layouts  1.41 us (1%)
    pallas_call x1, Pallas kernels, local(): pl.pallas_call(kernel, out_shape=(pltpu.VMEM(focus_plus.shape, BF),) * 2,...  93.7 us

profile of v3, /device:TPU:1, one launch (start us, length us, event | category | flops | bytes accessed | tf_op | source)
XLA Modules:
  0.0 95.8 jit_solution(2496056853727481247)
XLA Ops:
  0.6 93.7 %shard_map.77 = (bf16[2,2,128,256]{3,2,1,0:T(8,128)(2,1)S(1)}, bf16[2,2,128,256]{3,2,1,0:T(8,128)(2,1)S(1)}) custom-call(bf16[2,2,256,4096]{3,2,1,0:T(8,128)(2,1)} %refl_hbm.1, bf16[2,2,128,256]{3,2,1,0:T(8,128)(2,1)} %plus_hbm.1, bf16[2,2,128,256]{3,2,1,0:T(8,128)(2,1)} %direct_hbm.1, s32[128,256]{1,0:T(8,128)} %arrival_hbm.1, ...), custom_call_target="tpu_custom_call" | custom-call | tf_op jit(solution)/shard_map/pallas_call | solution.py:309
  94.3 0.7 copy.10
  95.1 0.7 copy.11
